TPU v7x, 128 devices: a whole 4x4x4 slice. The times are simulated.
128 devices in a mesh: dp: 16 (over y, z), expert: 8 (over x, core).
Axes of the slice: x: 4, y: 4, z: 4, core: 2. Of those that a mesh axis runs over, the one named last changes fastest.
Arguments:
- grad_out: bfloat16 [16384, 6144], P(('dp', 'expert')), may hold values from -6 to 6
- routes: int32 [16384, 2], P(('dp', 'expert')), may hold values from 0 to 31, all different within a row; in each aligned block of 128 rows (0 to 127, 128 to 255, ...) at most 9 rows name the same one
- loss_weight: int32 [16384], P(('dp', 'expert')), may hold values from 1 to 4
- saved_input: bfloat16 [32, 1152, 6144], P('dp', None, 'expert'), may hold values from -6 to 6
- saved_gate: bfloat16 [32, 1152, 1024], P('dp', None, 'expert'), may hold values from -8 to 8
- saved_up: bfloat16 [32, 1152, 1024], P('dp', None, 'expert'), may hold values from -6 to 6
- w_gate: bfloat16 [32, 6144, 1024], P('dp', 'expert'), may hold values from -0.1875 to 0.1875
- w_up: bfloat16 [32, 6144, 1024], P('dp', 'expert'), may hold values from -0.1875 to 0.1875
- w_down: bfloat16 [32, 1024, 6144], P('dp', None, 'expert'), may hold values from -0.078125 to 0.078125
Outputs:
- grad_input: bfloat16 [16384, 6144], P(('dp', 'expert'))
- grad_gate: bfloat16 [32, 6144, 1024], P('dp', 'expert')
- grad_up: bfloat16 [32, 6144, 1024], P('dp', 'expert')
- grad_down: bfloat16 [32, 1024, 6144], P('dp', None, 'expert')
Inputs may be any that keep to these rules, and one draw needn't show every extreme that they name: `routes`: each row names two different experts; among the rows of one device no expert is named more than 9 times, and some device names some expert exactly 9 times.
All inputs are finite; a program needn't handle non-finite values.
Results may differ from a plain program's by a relative error of at most 0.0061.
Values may be sent and summed in bfloat16 or wider, within the bound.
No kernel may reach another device: no remote copies, remote signals or barrier semaphores. Data moves between devices by JAX's collectives and lax.ppermute only.
A program may use at most 192 MiB of HBM per device.

v0:
```python
import jax
import jax.numpy as jnp
from jax import lax
from jax.sharding import PartitionSpec as P


def body(grad_out, routes, loss_weight, saved_input, saved_gate, saved_up, w_gate, w_up, w_down):
    groups = lax.axis_size("dp")
    splits = lax.axis_size("expert")
    local_experts = w_gate.shape[0]
    experts_all = local_experts * groups
    tokens_here = grad_out.shape[0]
    width = grad_out.shape[1]
    slice_width = width // splits
    slots_all = saved_input.shape[1]
    capacity = slots_all // (groups * splits)
    scaled = (
        grad_out.astype(jnp.float32) * loss_weight.astype(jnp.float32)[:, None] * 0.25
    ).astype(jnp.bfloat16)
    chosen = routes.reshape(-1)
    onehot = (chosen[:, None] == jnp.arange(experts_all, dtype=jnp.int32)[None, :]).astype(
        jnp.int32
    )
    before = jnp.cumsum(onehot, axis=0) - onehot
    rank = jnp.sum(before * onehot, axis=1)
    dest_row = (chosen % local_experts * groups + chosen // local_experts) * capacity + rank
    marks = (
        dest_row[:, None] == jnp.arange(experts_all * capacity, dtype=jnp.int32)[None, :]
    ).astype(jnp.float32)
    placed = jnp.sum(marks.reshape(tokens_here, 2, experts_all * capacity), axis=1).astype(
        jnp.bfloat16
    )
    outgoing = jnp.einsum("tr,td->rd", placed, scaled, preferred_element_type=jnp.float32).astype(
        jnp.bfloat16
    )
    ordered = outgoing.reshape(local_experts, groups, capacity, splits, slice_width)
    ordered = ordered.transpose(0, 1, 3, 2, 4).reshape(
        local_experts, groups * splits, capacity, slice_width
    )
    arrived = lax.all_to_all(ordered, ("dp", "expert"), split_axis=1, concat_axis=1, tiled=True)
    dispatched = arrived.reshape(local_experts, slots_all, slice_width)
    partial_value = jnp.einsum(
        "esd,ehd->esh", dispatched, w_down, preferred_element_type=jnp.float32
    )
    dhidden = lax.psum(partial_value, "expert")
    gates_all, ups_all = (
        lax.all_gather(saved_gate, "expert", axis=2, tiled=True),
        lax.all_gather(saved_up, "expert", axis=2, tiled=True),
    )
    gvals = gates_all.astype(jnp.float32)
    uvals = ups_all.astype(jnp.float32)
    sig = jax.nn.sigmoid(gvals)
    act = gvals * sig
    hidden = (act * uvals).astype(jnp.bfloat16)
    dgate = (dhidden * uvals * sig * (1.0 + gvals * (1.0 - sig))).astype(jnp.bfloat16)
    dup = (dhidden * act).astype(jnp.bfloat16)
    hidden, dgate, dup = (hidden, dgate, dup)
    grad_down = jnp.einsum(
        "esh,esd->ehd", hidden, dispatched, preferred_element_type=jnp.float32
    ).astype(jnp.bfloat16)
    grad_gate = jnp.einsum(
        "esd,esh->edh", saved_input, dgate, preferred_element_type=jnp.float32
    ).astype(jnp.bfloat16)
    grad_up = jnp.einsum(
        "esd,esh->edh", saved_input, dup, preferred_element_type=jnp.float32
    ).astype(jnp.bfloat16)
    slot_grad = jnp.einsum("esh,edh->esd", dgate, w_gate, preferred_element_type=jnp.float32)
    slot_grad = slot_grad + jnp.einsum(
        "esh,edh->esd", dup, w_up, preferred_element_type=jnp.float32
    )
    slot_grad = slot_grad.astype(jnp.bfloat16)
    leaving = slot_grad.reshape(local_experts, groups * splits, capacity, slice_width)
    returned = lax.all_to_all(leaving, ("dp", "expert"), split_axis=1, concat_axis=1, tiled=True)
    returned = returned.reshape(local_experts, groups, splits, capacity, slice_width).transpose(
        0, 1, 3, 2, 4
    )
    returned = returned.reshape(experts_all * capacity, width)
    grad_input = jnp.einsum(
        "tr,rd->td", placed, returned, preferred_element_type=jnp.float32
    ).astype(jnp.bfloat16)
    return (grad_input, grad_gate, grad_up, grad_down)


def solution(mesh):
    return jax.shard_map(
        body,
        mesh=mesh,
        in_specs=(
            P(("dp", "expert"), None),
            P(("dp", "expert"), None),
            P(("dp", "expert")),
            P("dp", None, "expert"),
            P("dp", None, "expert"),
            P("dp", None, "expert"),
            P("dp", "expert", None),
            P("dp", "expert", None),
            P("dp", None, "expert"),
        ),
        out_specs=(
            P(("dp", "expert"), None),
            P("dp", "expert", None),
            P("dp", "expert", None),
            P("dp", None, "expert"),
        ),
        check_vma=False,
    )
```

profile of v0, /device:TPU:1, one launch (start us, length us, event | category | flops | bytes accessed | tf_op | source)
XLA Modules:
  0.0 385.4 jit_solution(1867682180642988697)
XLA Ops:
  7.2 0.0 copy-start
  7.2 0.0 all-reduce.2.cloned.1.call-start
  7.2 1.6 copy.105
  8.8 1.0 eq.45
  9.8 1.0 eq.41
  10.7 0.7 convert_element_type.67
  11.4 0.6 fusion.25
  12.0 1.9 reduce-window.6
  13.9 0.9 slice_reduce_fusion
  14.9 0.9 fusion.24
  15.8 0.8 reduce_sum.21
  16.5 0.9 copy.108
  17.4 0.7 multiply_add_fusion
  18.2 0.0 copy-start.4
  18.2 2.6 convolution_convert_fusion
  20.8 0.0 copy-done.4
  20.8 1.0 copy.124
  21.8 0.4 copy.134
  22.3 3.6 copy.110
  25.9 0.0 copy-start.6
  25.9 57.3 %all_to_all.10 = bf16[2,128,9,768]{3,0,2,1:T(2,128)(2,1)S(1)} all-to-all(bf16[2,128,9,768]{3,0,2,1:T(2,128)(2,1)S(1)} %copy.110), channel_id=1, replica_groups=mesh['dp'=16,'expert'=8] {'dp','expert'}, dimensions={1} | all-to-all | bytes 7077888 | tf_op jit(solution)/shard_map/all_to_all | solution.py:40
  83.2 0.0 copy-start.3
  83.3 1.9 copy-done.3
  85.1 0.0 copy-done.6
  85.1 6.2 %fusion.11 = f32[2,1152,1024]{2,1,0:T(8,128)} fusion(bf16[2,1024,768]{2,1,0:T(8,128)(2,1)S(1)} %copy-done.6, bf16[2,1152,768]{2,0,1:T(2,128)(2,1)S(1)} %bitcast.56), kind=kOutput, calls=%fused_computation.23 | convolution fusion | flops 3623878656 | bytes 16121856 | tf_op jit(solution)/shard_map/esd,ehd->esh/dot_general | solution.py:42
  91.3 0.0 all-reduce.2.cloned.1.call-update
  91.3 0.0 all-gather.5.cloned.1.call-start
  91.4 0.7 all-gather.5.cloned.1.call-update
  92.1 0.2 all-gather.3.cloned.1.call-start
  92.3 0.5 all-gather.3.cloned.1.call-update
  92.8 108.4 %all-reduce.2.cloned.1.call-done = f32[2,1152,1024]{2,1,0:T(8,128)} async-done(((f32[2,1152,1024]{2,1,0:T(8,128)}), f32[2,1152,1024]{2,1,0:T(8,128)}) %all-reduce.2.cloned.1.call-update) | async-done | bytes 9437200 | tf_op jit(solution)/shard_map/psum | solution.py:45
  201.2 40.5 %all-gather.5.cloned.1.call-done = bf16[2,1152,1024]{2,1,0:T(8,128)(2,1)} async-done(((bf16[2,1152,128]{2,1,0:T(8,128)(2,1)}), bf16[2,1152,1024]{2,1,0:T(8,128)(2,1)}) %all-gather.5.cloned.1.call-update) | async-done | bytes 4718608 | tf_op jit(solution)/shard_map/all_gather | solution.py:47
  241.8 41.0 %all-gather.3.cloned.1.call-done = bf16[2,1152,1024]{2,1,0:T(8,128)(2,1)} async-done(((bf16[2,1152,128]{2,1,0:T(8,128)(2,1)}), bf16[2,1152,1024]{2,1,0:T(8,128)(2,1)}) %all-gather.3.cloned.1.call-update) | async-done | bytes 4718608 | tf_op jit(solution)/shard_map/all_gather | solution.py:48
  282.7 0.0 copy-start.7
  282.7 9.0 %multiply_convert_fusion = (bf16[2,1152,1024]{2,1,0:T(8,128)(2,1)S(1)}, bf16[2,1152,1024]{2,1,0:T(8,128)(2,1)S(1)}) fusion(f32[2,1152,1024]{2,1,0:T(8,128)} %all-reduce.2.cloned.1.call-done, bf16[2,1152,1024]{2,1,0:T(8,128)(2,1)} %all-gather.5.cloned.1.call-done, bf16[2,1152,1024]{2,1,0:T(8,128)(2,1)} %all-gather.3.cloned.1.call-done), kind=kLoop, calls=%fused_computation.13 | loop fusion | flops 35389440 | bytes 28311552 | tf_op jit(solution)/shard_map/convert_element_type | solution.py:56
  291.8 0.0 copy-start.1
  291.8 0.0 copy-start.2
  291.8 0.0 copy-done.7
  291.8 0.0 copy-start.8
  291.8 5.9 %fusion.30 = f32[2,1152,768]{2,1,0:T(8,128)} fusion(bf16[2,1152,1024]{2,1,0:T(8,128)(2,1)S(1)} %get-tuple-element.29, bf16[2,768,1024]{2,1,0:T(8,128)(2,1)S(1)} %copy-done.7), kind=kOutput, calls=%fused_computation.51 | convolution fusion | flops 3623878656 | bytes 14942208 | tf_op jit(solution)/shard_map/esh,edh->esd/dot_general | solution.py:67
  297.8 0.0 copy-done.1
  297.8 0.4 copy-done.2
  298.2 0.0 copy-done.8
  298.2 6.1 %add_convert_fusion = bf16[2,1152,768]{2,1,0:T(8,128)(2,1)S(1)} fusion(f32[2,1152,768]{2,1,0:T(8,128)} %fusion.30, bf16[2,1152,1024]{2,1,0:T(8,128)(2,1)S(1)} %get-tuple-element.28, bf16[2,768,1024]{2,1,0:T(8,128)(2,1)S(1)} %copy-done.8), kind=kOutput, calls=%fused_computation.16 | convolution fusion | flops 3627417600 | bytes 18481152 | tf_op jit(solution)/shard_map/esh,edh->esd/dot_general | solution.py:68
  304.3 13.9 %copy.112 = bf16[2,1152,768]{2,0,1:T(2,128)(2,1)} copy(bf16[2,1152,768]{2,1,0:T(8,128)(2,1)S(1)} %add_convert_fusion) | data formatting | bytes 7077888 | tf_op jit(solution)/shard_map/convert_element_type | solution.py:71
  318.2 9.3 %all-to-all-start.1 = ((bf16[2,128,9,768]{3,0,2,1:T(2,128)(2,1)}), bf16[2,128,9,768]{3,0,2,1:T(2,128)(2,1)}, u32[]{:S(2)}, u32[]{:S(2)}) async-start(bf16[2,128,9,768]{3,0,2,1:T(2,128)(2,1)} %bitcast.52), calls=%async_computation.1 | async-start | bytes 7077888 | tf_op jit(solution)/shard_map/all_to_all | solution.py:73
  327.5 0.0 copy-done
  327.5 9.4 %convert_bitcast_fusion = bf16[2,768,1024]{1,2,0:T(8,128)(2,1)} fusion(bf16[2,1152,1024]{2,1,0:T(8,128)(2,1)} %copy-done.2, bf16[2,1152,768]{2,1,0:T(8,128)(2,1)S(1)} %copy-done), kind=kOutput, calls=%fused_computation.19 | convolution fusion | flops 3625451520 | bytes 11403264 | tf_op jit(solution)/shard_map/esd,esh->edh/dot_general | solution.py:64
  337.0 4.6 %copy.119 = bf16[2,768,1024]{2,1,0:T(8,128)(2,1)} copy(bf16[2,768,1024]{1,2,0:T(8,128)(2,1)} %convert_bitcast_fusion) | data formatting | bytes 6291456
  341.6 9.4 %convert_bitcast_fusion.1 = bf16[2,768,1024]{1,2,0:T(8,128)(2,1)} fusion(bf16[2,1152,1024]{2,1,0:T(8,128)(2,1)} %copy-done.1, bf16[2,1152,768]{2,1,0:T(8,128)(2,1)S(1)} %copy-done), kind=kOutput, calls=%fused_computation.20 | convolution fusion | flops 3625451520 | bytes 11403264 | tf_op jit(solution)/shard_map/esd,esh->edh/dot_general | solution.py:61
  351.0 4.6 %copy.118 = bf16[2,768,1024]{2,1,0:T(8,128)(2,1)} copy(bf16[2,768,1024]{1,2,0:T(8,128)(2,1)} %convert_bitcast_fusion.1) | data formatting | bytes 6291456
  355.6 12.1 %fusion.13 = bf16[2,1024,768]{2,1,0:T(8,128)(2,1)} fusion(bf16[2,1152,768]{2,0,1:T(2,128)(2,1)} %bitcast.57, bf16[2,1152,1024]{2,1,0:T(8,128)(2,1)} %all-gather.3.cloned.1.call-done, bf16[2,1152,1024]{2,1,0:T(8,128)(2,1)} %all-gather.5.cloned.1.call-done), kind=kOutput, calls=%fused_computation.25 | convolution fusion | flops 3644325888 | bytes 16121856 | tf_op jit(solution)/shard_map/esh,esd->ehd/dot_general | solution.py:58
  367.8 5.5 %all-to-all-done.1 = bf16[2,128,9,768]{3,0,2,1:T(2,128)(2,1)} async-done(((bf16[2,128,9,768]{3,0,2,1:T(2,128)(2,1)}), bf16[2,128,9,768]{3,0,2,1:T(2,128)(2,1)}, u32[]{:S(2)}, u32[]{:S(2)}) %all-to-all-start.1) | async-done | bytes 3538976 | tf_op jit(solution)/shard_map/all_to_all | solution.py:73
  373.2 2.5 copy.113
  375.7 0.0 copy-start.5
  375.7 1.0 copy.125
  376.7 0.0 copy-done.5
  376.7 2.2 convolution_convert_fusion.1
  (3 shorter events, 0.1 us)
Async XLA Ops:
  7.2 320.4 %copy-start = (bf16[2,1152,768]{2,1,0:T(8,128)(2,1)S(1)}, bf16[2,1152,768]{2,1,0:T(8,128)(2,1)}, u32[]{:S(2)}) copy-start(bf16[2,1152,768]{2,1,0:T(8,128)(2,1)} %param.12) | copy-start | bytes 10616836
  7.2 194.1 %all-reduce.2.cloned.1.call-start = ((), (), s32[]{:S(2)}) async-start(), calls=%async_computation.2 | async-start | bytes 18874368 | tf_op jit(solution)/shard_map/psum | solution.py:45
  18.2 2.6 copy-start.4
  25.9 59.2 %copy-start.6 = (bf16[2,1024,768]{2,1,0:T(8,128)(2,1)S(1)}, bf16[2,1024,768]{2,1,0:T(8,128)(2,1)}, u32[]{:S(2)}) copy-start(bf16[2,1024,768]{2,1,0:T(8,128)(2,1)} %param.17) | copy-start | bytes 9437188
  83.2 1.9 copy-start.3
  91.3 150.4 %all-gather.5.cloned.1.call-start = ((), (), s32[]{:S(2)}) async-start(), calls=%async_computation.4 | async-start | bytes 5308416 | tf_op jit(solution)/shard_map/all_gather | solution.py:47
  92.1 190.6 %all-gather.3.cloned.1.call-start = ((), (), s32[]{:S(2)}) async-start(), calls=%async_computation.3 | async-start | bytes 5308416 | tf_op jit(solution)/shard_map/all_gather | solution.py:48
  282.7 9.1 %copy-start.7 = (bf16[2,768,1024]{2,1,0:T(8,128)(2,1)S(1)}, bf16[2,768,1024]{2,1,0:T(8,128)(2,1)}, u32[]{:S(2)}) copy-start(bf16[2,768,1024]{2,1,0:T(8,128)(2,1)} %param.15) | copy-start | bytes 9437188
  291.8 6.0 %copy-start.1 = (bf16[2,1152,1024]{2,1,0:T(8,128)(2,1)}, bf16[2,1152,1024]{2,1,0:T(8,128)(2,1)S(1)}, u32[]{:S(2)}) copy-start(bf16[2,1152,1024]{2,1,0:T(8,128)(2,1)S(1)} %get-tuple-element.29) | copy-start | bytes 14155780
  291.8 6.4 %copy-start.2 = (bf16[2,1152,1024]{2,1,0:T(8,128)(2,1)}, bf16[2,1152,1024]{2,1,0:T(8,128)(2,1)S(1)}, u32[]{:S(2)}) copy-start(bf16[2,1152,1024]{2,1,0:T(8,128)(2,1)S(1)} %get-tuple-element.28) | copy-start | bytes 14155780
  291.8 6.4 %copy-start.8 = (bf16[2,768,1024]{2,1,0:T(8,128)(2,1)S(1)}, bf16[2,768,1024]{2,1,0:T(8,128)(2,1)}, u32[]{:S(2)}) copy-start(bf16[2,768,1024]{2,1,0:T(8,128)(2,1)} %param.16) | copy-start | bytes 9437188
  318.2 55.0 %all-to-all-start.1 = ((bf16[2,128,9,768]{3,0,2,1:T(2,128)(2,1)}), bf16[2,128,9,768]{3,0,2,1:T(2,128)(2,1)}, u32[]{:S(2)}, u32[]{:S(2)}) async-start(bf16[2,128,9,768]{3,0,2,1:T(2,128)(2,1)} %bitcast.52), calls=%async_computation.1 | async-start | bytes 7077888 | tf_op jit(solution)/shard_map/all_to_all | solution.py:73
  375.7 1.0 copy-start.5
Sparse Core Ops, SparseCore 0:
  91.5 109.7 all-reduce.1
  202.9 38.8 all-gather.4
  243.5 39.2 all-gather.2
where the time goes:
time: 386 us; the launch traced here: 385 us
  waiting for transfers between devices  197 us (51%)
  blocking collectives  57.3 us (15%)
  matrix products  54 us (14%)
  local copies, waits for them, and re-layouts  40.1 us (10%)
  other arithmetic  13.9 us (4%)
  between operations  13.9 us (4%)
  starting transfers between devices  9.56 us (2%)
    psum x1, waiting for transfers between devices, body(): dhidden = lax.psum(partial_value, 'expert')  108 us
    all_to_all x1, blocking collectives, body(): lax.all_to_all(ordered, ('dp', 'expert'), split_axis=1, concat_axis=1, ti...  57.3 us
    all_gather x1, waiting for transfers between devices, body(): lax.all_gather(saved_up, 'expert', axis=2, tiled=True)  41 us
    all_gather x1, waiting for transfers between devices, body(): lax.all_gather(saved_gate, 'expert', axis=2, tiled=True)  40.5 us
    unnamed x23, local copies, waits for them, and re-layouts  15.2 us
    convert_element_type x1, local copies, waits for them, and re-layouts, body(): slot_grad = slot_grad.astype(jnp.bfloat16)  13.9 us
    dot_general x1, matrix products, body(): jnp.einsum('esh,esd->ehd', hidden, dispatched, preferred_element_type=jnp...  12.1 us
    dot_general x1, matrix products, body(): jnp.einsum('esd,esh->edh', saved_input, dup, preferred_element_type=jnp.f...  9.43 us
  transfers between devices with their start and end apart: 4, of which 4 were waited for; matrix products, arithmetic and copies ran while one was open for 10% of the time, Pallas kernels for 0%

commit v1 on v0

--- a/solution.py
+++ b/solution.py
@@ -43,8 +43,19 @@
         "esd,ehd->esh", dispatched, w_down, preferred_element_type=jnp.float32
     )
     dhidden = lax.psum(partial_value, "expert")
+
+    def close_gates(load, named_axis):
+        buffer = []
+        for _ in range(lax.axis_size(named_axis)):
+            buffer.append(load)
+        local_out = lax.all_to_all(
+            jnp.stack(buffer, axis=0), axis_name=named_axis, split_axis=0, concat_axis=0
+        )
+        earlier = jnp.concatenate(local_out, axis=2)
+        return earlier
+
     gates_all, ups_all = (
-        lax.all_gather(saved_gate, "expert", axis=2, tiled=True),
+        close_gates(saved_gate, "expert"),
         lax.all_gather(saved_up, "expert", axis=2, tiled=True),
     )
     gvals = gates_all.astype(jnp.float32)

time: 386 us -> 395 us (1.023)
  blocking collectives: 57.3 us -> 141 us
  waiting for transfers between devices: 197 us -> 119 us
    all_to_all x0 -> x1, blocking collectives: none -> 84.1 us  [close_gates(): lax.all_to_all(jnp.stack(buffer, axis=0), axis_name=named_axis, split_axi...]
    all_gather x1 -> x0, waiting for transfers between devices: 40.5 us -> none  [body(): lax.all_gather(saved_gate, 'expert', axis=2, tiled=True)]
    psum x1, waiting for transfers between devices: 108 us -> 72 us  [body(): dhidden = lax.psum(partial_value, 'expert')]
  transfers between devices with their start and end apart: 4 -> 3, of which waited for: 4 -> 3; matrix products, arithmetic and copies ran while one was open for 10% -> 11% of each run, Pallas kernels for 0% -> 0%
where the time goes in v1:
time: 395 us; the launch traced here: 394 us
  blocking collectives  141 us (36%)
  waiting for transfers between devices  119 us (30%)
  matrix products  54 us (14%)
  local copies, waits for them, and re-layouts  42.1 us (11%)
  between operations  14.2 us (4%)
  other arithmetic  13.9 us (4%)
  starting transfers between devices  9.34 us (2%)
    all_to_all x1, blocking collectives, close_gates(): lax.all_to_all(jnp.stack(buffer, axis=0), axis_name=named_axis, split_axi...  84.1 us
    psum x1, waiting for transfers between devices, body(): dhidden = lax.psum(partial_value, 'expert')  72 us
    all_to_all x1, blocking collectives, body(): lax.all_to_all(ordered, ('dp', 'expert'), split_axis=1, concat_axis=1, ti...  57.3 us
    all_gather x1, waiting for transfers between devices, body(): lax.all_gather(saved_up, 'expert', axis=2, tiled=True)  40.5 us
    unnamed x23, local copies, waits for them, and re-layouts  15.2 us
    convert_element_type x1, local copies, waits for them, and re-layouts, body(): slot_grad = slot_grad.astype(jnp.bfloat16)  13.9 us
    dot_general x1, matrix products, body(): jnp.einsum('esh,esd->ehd', hidden, dispatched, preferred_element_type=jnp...  12.1 us
    dot_general x1, matrix products, body(): jnp.einsum('esd,esh->edh', saved_input, dup, preferred_element_type=jnp.f...  9.43 us
  transfers between devices with their start and end apart: 3, of which 3 were waited for; matrix products, arithmetic and copies ran while one was open for 11% of the time, Pallas kernels for 0%

profile of v1, /device:TPU:1, one launch (start us, length us, event | category | flops | bytes accessed | tf_op | source)
XLA Modules:
  0.0 393.7 jit_solution(14988881456168106648)
XLA Ops:
  7.2 0.0 copy-start
  7.2 0.0 all-reduce.2.cloned.1.call-start
  7.2 1.6 copy.108
  8.8 1.0 eq.45
  9.8 1.0 eq.41
  10.7 0.7 convert_element_type.73
  11.4 0.6 fusion.25
  12.0 1.9 reduce-window.6
  13.9 0.9 slice_reduce_fusion
  14.9 0.9 fusion.24
  15.8 0.8 reduce_sum.21
  16.5 0.9 copy.111
  17.4 0.7 multiply_add_fusion
  18.2 0.0 copy-start.4
  18.2 2.6 convolution_convert_fusion
  20.8 0.0 copy-done.4
  20.8 1.0 copy.129
  21.8 0.4 copy.146
  22.3 3.6 copy.113
  25.9 0.0 copy-start.6
  25.9 57.3 %all_to_all.15 = bf16[2,128,9,768]{3,0,2,1:T(2,128)(2,1)S(1)} all-to-all(bf16[2,128,9,768]{3,0,2,1:T(2,128)(2,1)S(1)} %copy.113), channel_id=1, replica_groups=mesh['dp'=16,'expert'=8] {'dp','expert'}, dimensions={1} | all-to-all | bytes 7077888 | tf_op jit(solution)/shard_map/all_to_all | solution.py:40
  83.2 0.0 copy-start.3
  83.3 1.9 copy-done.3
  85.1 0.0 copy-done.6
  85.1 6.2 %fusion.11 = f32[2,1152,1024]{2,1,0:T(8,128)} fusion(bf16[2,1024,768]{2,1,0:T(8,128)(2,1)S(1)} %copy-done.6, bf16[2,1152,768]{2,0,1:T(2,128)(2,1)S(1)} %bitcast.85), kind=kOutput, calls=%fused_computation.24 | convolution fusion | flops 3623878656 | bytes 16121856 | tf_op jit(solution)/shard_map/esd,ehd->esh/dot_general | solution.py:42
  91.3 0.0 all-reduce.2.cloned.1.call-update
  91.4 0.0 all-gather.2.cloned.1.call-start
  91.4 0.7 all-gather.2.cloned.1.call-update
  92.1 2.0 stack.2
  94.1 84.1 %all_to_all.16 = bf16[8,2,1152,128]{3,2,1,0:T(8,128)(2,1)} all-to-all(bf16[8,2,1152,128]{3,2,1,0:T(8,128)(2,1)S(1)} %stack.2), channel_id=1, replica_groups=mesh['dp'=16,'expert'=8] {'expert'}, dimensions={0} | all-to-all | bytes 9437184 | tf_op jit(solution)/shard_map/all_to_all | solution.py:51
  178.2 72.0 %all-reduce.2.cloned.1.call-done = f32[2,1152,1024]{2,1,0:T(8,128)} async-done(((f32[2,1152,1024]{2,1,0:T(8,128)}), f32[2,1152,1024]{2,1,0:T(8,128)}) %all-reduce.2.cloned.1.call-update) | async-done | bytes 9437200 | tf_op jit(solution)/shard_map/psum | solution.py:45
  250.1 40.5 %all-gather.2.cloned.1.call-done = bf16[2,1152,1024]{2,1,0:T(8,128)(2,1)} async-done(((bf16[2,1152,128]{2,1,0:T(8,128)(2,1)}), bf16[2,1152,1024]{2,1,0:T(8,128)(2,1)}) %all-gather.2.cloned.1.call-update) | async-done | bytes 4718608 | tf_op jit(solution)/shard_map/all_gather | solution.py:59
  290.7 0.0 copy-start.7
  290.7 9.0 %multiply_convert_fusion = (bf16[2,1152,1024]{2,1,0:T(8,128)(2,1)S(1)}, bf16[2,1152,1024]{2,1,0:T(8,128)(2,1)S(1)}) fusion(f32[2,1152,1024]{2,1,0:T(8,128)} %all-reduce.2.cloned.1.call-done, bf16[2,1152,1024]{2,1,0:T(8,128)(2,1)} %all-gather.2.cloned.1.call-done, bf16[8,2,1152,128]{3,2,1,0:T(8,128)(2,1)} %all_to_all.16), kind=kLoop, calls=%fused_computation.14 | loop fusion | flops 35389440 | bytes 28311552 | tf_op jit(solution)/shard_map/convert_element_type | solution.py:67
  299.7 0.0 copy-start.1
  299.7 0.0 copy-start.2
  299.7 0.0 copy-done.7
  299.7 0.0 copy-start.8
  299.8 5.9 %fusion.30 = f32[2,1152,768]{2,1,0:T(8,128)} fusion(bf16[2,1152,1024]{2,1,0:T(8,128)(2,1)S(1)} %get-tuple-element.29, bf16[2,768,1024]{2,1,0:T(8,128)(2,1)S(1)} %copy-done.7), kind=kOutput, calls=%fused_computation.52 | convolution fusion | flops 3623878656 | bytes 14942208 | tf_op jit(solution)/shard_map/esh,edh->esd/dot_general | solution.py:78
  305.7 0.0 copy-done.1
  305.7 0.4 copy-done.2
  306.1 0.0 copy-done.8
  306.1 6.1 %add_convert_fusion = bf16[2,1152,768]{2,1,0:T(8,128)(2,1)S(1)} fusion(f32[2,1152,768]{2,1,0:T(8,128)} %fusion.30, bf16[2,1152,1024]{2,1,0:T(8,128)(2,1)S(1)} %get-tuple-element.28, bf16[2,768,1024]{2,1,0:T(8,128)(2,1)S(1)} %copy-done.8), kind=kOutput, calls=%fused_computation.17 | convolution fusion | flops 3627417600 | bytes 18481152 | tf_op jit(solution)/shard_map/esh,edh->esd/dot_general | solution.py:79
  312.2 13.9 %copy.116 = bf16[2,1152,768]{2,0,1:T(2,128)(2,1)} copy(bf16[2,1152,768]{2,1,0:T(8,128)(2,1)S(1)} %add_convert_fusion) | data formatting | bytes 7077888 | tf_op jit(solution)/shard_map/convert_element_type | solution.py:82
  326.2 9.3 %all-to-all-start.2 = ((bf16[2,128,9,768]{3,0,2,1:T(2,128)(2,1)}), bf16[2,128,9,768]{3,0,2,1:T(2,128)(2,1)}, u32[]{:S(2)}, u32[]{:S(2)}) async-start(bf16[2,128,9,768]{3,0,2,1:T(2,128)(2,1)} %bitcast.81), calls=%async_computation.2 | async-start | bytes 7077888 | tf_op jit(solution)/shard_map/all_to_all | solution.py:84
  335.4 0.0 copy-done
  335.5 9.4 %convert_bitcast_fusion.1 = bf16[2,768,1024]{1,2,0:T(8,128)(2,1)} fusion(bf16[2,1152,1024]{2,1,0:T(8,128)(2,1)} %copy-done.2, bf16[2,1152,768]{2,1,0:T(8,128)(2,1)S(1)} %copy-done), kind=kOutput, calls=%fused_computation.20 | convolution fusion | flops 3625451520 | bytes 11403264 | tf_op jit(solution)/shard_map/esd,esh->edh/dot_general | solution.py:75
  344.9 4.6 %copy.123 = bf16[2,768,1024]{2,1,0:T(8,128)(2,1)} copy(bf16[2,768,1024]{1,2,0:T(8,128)(2,1)} %convert_bitcast_fusion.1) | data formatting | bytes 6291456
  349.5 9.4 %convert_bitcast_fusion.2 = bf16[2,768,1024]{1,2,0:T(8,128)(2,1)} fusion(bf16[2,1152,1024]{2,1,0:T(8,128)(2,1)} %copy-done.1, bf16[2,1152,768]{2,1,0:T(8,128)(2,1)S(1)} %copy-done), kind=kOutput, calls=%fused_computation.21 | convolution fusion | flops 3625451520 | bytes 11403264 | tf_op jit(solution)/shard_map/esd,esh->edh/dot_general | solution.py:72
  359.0 4.6 %copy.122 = bf16[2,768,1024]{2,1,0:T(8,128)(2,1)} copy(bf16[2,768,1024]{1,2,0:T(8,128)(2,1)} %convert_bitcast_fusion.2) | data formatting | bytes 6291456
  363.6 12.1 %fusion.13 = bf16[2,1024,768]{2,1,0:T(8,128)(2,1)} fusion(bf16[2,1152,768]{2,0,1:T(2,128)(2,1)} %bitcast.86, bf16[2,1152,1024]{2,1,0:T(8,128)(2,1)} %all-gather.2.cloned.1.call-done, bf16[8,2,1152,128]{3,2,1,0:T(8,128)(2,1)} %all_to_all.16), kind=kOutput, calls=%fused_computation.26 | convolution fusion | flops 3644325888 | bytes 16121856 | tf_op jit(solution)/shard_map/esh,esd->ehd/dot_general | solution.py:69
  375.7 5.5 %all-to-all-done.2 = bf16[2,128,9,768]{3,0,2,1:T(2,128)(2,1)} async-done(((bf16[2,128,9,768]{3,0,2,1:T(2,128)(2,1)}), bf16[2,128,9,768]{3,0,2,1:T(2,128)(2,1)}, u32[]{:S(2)}, u32[]{:S(2)}) %all-to-all-start.2) | async-done | bytes 3538976 | tf_op jit(solution)/shard_map/all_to_all | solution.py:84
  381.2 2.5 copy.117
  383.6 0.0 copy-start.5
  383.6 1.0 copy.130
  384.7 0.0 copy-done.5
  384.7 2.2 convolution_convert_fusion.1
  (3 shorter events, 0.1 us)
Async XLA Ops:
  7.2 328.3 %copy-start = (bf16[2,1152,768]{2,1,0:T(8,128)(2,1)S(1)}, bf16[2,1152,768]{2,1,0:T(8,128)(2,1)}, u32[]{:S(2)}) copy-start(bf16[2,1152,768]{2,1,0:T(8,128)(2,1)} %param.12) | copy-start | bytes 10616836
  7.2 242.9 %all-reduce.2.cloned.1.call-start = ((), (), s32[]{:S(2)}) async-start(), calls=%async_computation.3 | async-start | bytes 18874368 | tf_op jit(solution)/shard_map/psum | solution.py:45
  18.2 2.6 copy-start.4
  25.9 59.2 %copy-start.6 = (bf16[2,1024,768]{2,1,0:T(8,128)(2,1)S(1)}, bf16[2,1024,768]{2,1,0:T(8,128)(2,1)}, u32[]{:S(2)}) copy-start(bf16[2,1024,768]{2,1,0:T(8,128)(2,1)} %param.17) | copy-start | bytes 9437188
  83.2 1.9 copy-start.3
  91.4 199.3 %all-gather.2.cloned.1.call-start = ((), (), s32[]{:S(2)}) async-start(), calls=%async_computation.4 | async-start | bytes 5308416 | tf_op jit(solution)/shard_map/all_gather | solution.py:59
  290.7 9.1 %copy-start.7 = (bf16[2,768,1024]{2,1,0:T(8,128)(2,1)S(1)}, bf16[2,768,1024]{2,1,0:T(8,128)(2,1)}, u32[]{:S(2)}) copy-start(bf16[2,768,1024]{2,1,0:T(8,128)(2,1)} %param.15) | copy-start | bytes 9437188
  299.7 6.0 %copy-start.1 = (bf16[2,1152,1024]{2,1,0:T(8,128)(2,1)}, bf16[2,1152,1024]{2,1,0:T(8,128)(2,1)S(1)}, u32[]{:S(2)}) copy-start(bf16[2,1152,1024]{2,1,0:T(8,128)(2,1)S(1)} %get-tuple-element.29) | copy-start | bytes 14155780
  299.7 6.4 %copy-start.2 = (bf16[2,1152,1024]{2,1,0:T(8,128)(2,1)}, bf16[2,1152,1024]{2,1,0:T(8,128)(2,1)S(1)}, u32[]{:S(2)}) copy-start(bf16[2,1152,1024]{2,1,0:T(8,128)(2,1)S(1)} %get-tuple-element.28) | copy-start | bytes 14155780
  299.7 6.4 %copy-start.8 = (bf16[2,768,1024]{2,1,0:T(8,128)(2,1)S(1)}, bf16[2,768,1024]{2,1,0:T(8,128)(2,1)}, u32[]{:S(2)}) copy-start(bf16[2,768,1024]{2,1,0:T(8,128)(2,1)} %param.16) | copy-start | bytes 9437188
  326.2 55.0 %all-to-all-start.2 = ((bf16[2,128,9,768]{3,0,2,1:T(2,128)(2,1)}), bf16[2,128,9,768]{3,0,2,1:T(2,128)(2,1)}, u32[]{:S(2)}, u32[]{:S(2)}) async-start(bf16[2,128,9,768]{3,0,2,1:T(2,128)(2,1)} %bitcast.81), calls=%async_computation.2 | async-start | bytes 7077888 | tf_op jit(solution)/shard_map/all_to_all | solution.py:84
  383.6 1.0 copy-start.5
Sparse Core Ops, SparseCore 0:
  91.5 158.5 all-reduce.1
  251.8 38.8 all-gather.1
